TPU v7x, 32 devices: a whole 2x2x4 slice. The times are simulated.
32 devices in a mesh: shard: 4 (over y, x), replica: 8 (over z, core).
Axes of the slice: x: 2, y: 2, z: 4, core: 2. Of those that a mesh axis runs over, the one named last changes fastest.
Arguments:
- tokens: bfloat16 [2, 8, 1024, 2048], P(None, 'replica', 'shard'), may hold values from -6 to 6
- gain_attn: bfloat16 [2048], P('shard'), may hold values from 0.099609375 to 1.8984375
- w_query: bfloat16 [2048, 2048], P('shard'), may hold values from -0.5 to 0.5
- w_key: bfloat16 [512, 2048], P('shard'), may hold values from -0.5 to 0.5
- w_value: bfloat16 [512, 2048], P('shard'), may hold values from -0.125 to 0.125
- w_out: bfloat16 [2048, 2048], P('shard'), may hold values from -2 to 2
- gain_ff: bfloat16 [2048], P('shard'), may hold values from 0.099609375 to 1.8984375
- w_gate: bfloat16 [8192, 2048], P('shard'), may hold values from -0.125 to 0.125
- w_up: bfloat16 [8192, 2048], P('shard'), may hold values from -0.125 to 0.125
- w_down: bfloat16 [8192, 2048], P('shard'), may hold values from -0.25 to 0.25
- cotangent: bfloat16 [2, 8, 1024, 2048], P(None, 'replica', 'shard'), may hold values from -6 to 6
- segment_ids: int32 [2, 8, 1024], P(None, 'replica', 'shard'), may hold values from 0 to 12, as said below
- parents: int32 [2, 8, 13], P(None, 'replica'), may hold values from 0 to 4, as said below
Outputs:
- output: bfloat16 [2, 8, 1024, 2048], P(None, 'replica', 'shard')
- input_grad: float32 [2, 8, 1024, 2048], P(None, 'replica', 'shard')
- grad_gain_attn: float32 [2048], P('shard')
- grad_query: float32 [2048, 2048], P('shard')
- grad_key: float32 [512, 2048], P('shard')
- grad_value: float32 [512, 2048], P('shard')
- grad_out: float32 [2048, 2048], P('shard')
- grad_gain_ff: float32 [2048], P('shard')
- grad_gate: float32 [8192, 2048], P('shard')
- grad_up: float32 [8192, 2048], P('shard')
- grad_down: float32 [8192, 2048], P('shard')
Inputs may be any that keep to these rules, and one draw needn't show every extreme that they name: `segment_ids`: segment numbers never fall along a tree, begin at 0 (the trunk), and each of the 13 segments holds one token or more. `parents`: segment 0 is its own parent; segments 1 to 4 are children of segment 0; each later segment is a child of one of segments 1 to 4, and every one of those has a child.
All inputs are finite; a program needn't handle non-finite values.
Results may differ from a plain program's by a relative error of at most 0.02.
Values may be sent and summed in bfloat16 or wider, within the bound.
A program may use at most 384 MiB of HBM per device.

v0:
```python
import math
import jax
import jax.numpy as jnp
from jax import lax
from jax.sharding import PartitionSpec as P

HEADS = 32
KV_HEADS = 8
HEAD_DIM = 64
EPSILON = 1e-05
RESIDUAL = 0.22
ATTN_SCALE = 0.015625
ROPE_BASE = 10000000.0
NEGATIVE = -1e30


def tree_layout(segment_row, parent_row):
    seg_numbers = jnp.arange(parent_row.shape[0], dtype=jnp.int32)
    member = (segment_row[:, None] == seg_numbers[None, :]).astype(jnp.int32)
    lengths = jnp.sum(member, axis=0)
    starts = jnp.cumsum(lengths) - lengths
    parent_hit = parent_row[:, None] == seg_numbers[None, :]
    grandparent = jnp.sum(jnp.where(parent_hit, parent_row[None, :], 0), axis=1)
    itself = seg_numbers[:, None] == seg_numbers[None, :]
    related = itself | parent_hit | (grandparent[:, None] == seg_numbers[None, :])
    before = jnp.sum(jnp.where(related & jnp.logical_not(itself), lengths[None, :], 0), axis=1)
    position = jnp.arange(segment_row.shape[0], dtype=jnp.int32) + jnp.dot(member, before - starts)
    return (position, related.astype(jnp.int32), member)


def rotate(values, position, sign):
    half = values.shape[-1] // 2
    fraction = jnp.arange(half, dtype=jnp.float32) * (2.0 / values.shape[-1])
    freq = jnp.exp(-math.log(ROPE_BASE) * fraction)
    angle = position.astype(jnp.float32)[:, None] * freq[None, :]
    cosine = jnp.concatenate([jnp.cos(angle), jnp.cos(angle)], axis=-1)[:, None, :]
    sine = jnp.concatenate([jnp.sin(angle), jnp.sin(angle)], axis=-1)[:, None, :]
    turned = jnp.concatenate([-values[..., half:], values[..., :half]], axis=-1)
    return values * cosine + sign * turned * sine


def contract_last(left, right):
    return lax.dot_general(
        left, right, (((1,), (1,)), ((), ())), preferred_element_type=jnp.float32
    )


def contract_first(left, right):
    return lax.dot_general(
        left, right, (((0,), (0,)), ((), ())), preferred_element_type=jnp.float32
    )


def norm_back(values, scale, gain, grad_in):
    scaled = values * scale
    weighted = grad_in * gain
    back = scale * (weighted - scaled * jnp.mean(weighted * scaled, axis=-1, keepdims=True))
    return (back, jnp.sum(grad_in * scaled, axis=0))


def block_mask(member, related, begin, block_rows):
    member_block = lax.slice_in_dim(member, begin, begin + block_rows, axis=0)
    link = jnp.dot(jnp.dot(member_block, related), member.T)
    query_index = begin + jnp.arange(block_rows, dtype=jnp.int32)
    key_index = jnp.arange(member.shape[0], dtype=jnp.int32)
    return ((link > 0) & (key_index[None, :] <= query_index[:, None]))[None, None]


def body(
    tokens,
    gain_attn,
    w_query,
    w_key,
    w_value,
    w_out,
    gain_ff,
    w_gate,
    w_up,
    w_down,
    cotangent,
    segment_ids,
    parents,
):
    width = tokens.shape[3]
    group = HEADS // KV_HEADS
    all_segments = lax.all_gather(segment_ids, "shard", axis=2, tiled=True)
    tree_rows = all_segments.shape[2]
    block_rows = min(512, tree_rows)
    sums = [
        jnp.zeros(w.shape, jnp.float32)
        for w in (gain_attn, w_query, w_key, w_value, w_out, gain_ff, w_gate, w_up, w_down)
    ]
    gains = (
        lax.all_gather(gain_attn, "shard", axis=0, tiled=True),
        lax.all_gather(gain_ff, "shard", axis=0, tiled=True),
    )
    gain_first = gains[0].astype(jnp.float32)
    gain_second = gains[1].astype(jnp.float32)
    gain_attn_acc = jnp.zeros((width,), jnp.float32)
    gain_ff_acc = jnp.zeros((width,), jnp.float32)
    results = []
    input_grads = []
    for batch_index in range(tokens.shape[0]):
        inputs = tokens[batch_index, 0].astype(jnp.float32)
        position_all, related, member = tree_layout(
            all_segments[batch_index, 0], parents[batch_index, 0]
        )
        scale_first = lax.rsqrt(jnp.mean(inputs * inputs, axis=-1, keepdims=True) + EPSILON)
        normed = (inputs * scale_first * gain_first).astype(jnp.bfloat16)
        normed_all = lax.all_gather(normed, "shard", axis=0, tiled=True)
        own_heads = w_key.shape[0] // HEAD_DIM
        query_h = rotate(
            contract_last(normed_all, w_query).reshape(tree_rows, own_heads * group, HEAD_DIM),
            position_all,
            1.0,
        )
        query_h = query_h.astype(jnp.bfloat16).reshape(tree_rows, own_heads, group, HEAD_DIM)
        key_h = rotate(
            contract_last(normed_all, w_key).reshape(tree_rows, own_heads, HEAD_DIM),
            position_all,
            1.0,
        ).astype(jnp.bfloat16)
        value_h = (
            contract_last(normed_all, w_value)
            .astype(jnp.bfloat16)
            .reshape(tree_rows, own_heads, HEAD_DIM)
        )
        masks = []
        log_totals = []
        pieces = []
        for begin in range(0, tree_rows, block_rows):
            allowed_blk = block_mask(member, related, begin, block_rows)
            query_blk = query_h[begin : begin + block_rows]
            scores = (
                jnp.einsum("qhgd,khd->hgqk", query_blk, key_h, preferred_element_type=jnp.float32)
                * ATTN_SCALE
            )
            masked = jnp.where(allowed_blk, scores, NEGATIVE)
            top = jnp.max(masked, axis=-1, keepdims=True)
            expo = jnp.exp(masked - top)
            total = jnp.sum(expo, axis=-1, keepdims=True)
            masks.append(allowed_blk)
            log_totals.append(top + jnp.log(total))
            probs_low = (expo / total).astype(jnp.bfloat16)
            mixed = jnp.einsum(
                "hgqk,khd->qhgd", probs_low, value_h, preferred_element_type=jnp.float32
            )
            pieces.append(mixed.reshape(block_rows, own_heads * group * HEAD_DIM))
        attended_h = jnp.concatenate(pieces, axis=0).astype(jnp.bfloat16)
        attn_branch = lax.psum_scatter(
            jnp.dot(attended_h, w_out, preferred_element_type=jnp.float32),
            "shard",
            scatter_dimension=0,
            tiled=True,
        )
        middle = inputs + RESIDUAL * attn_branch
        scale_second = lax.rsqrt(jnp.mean(middle * middle, axis=-1, keepdims=True) + EPSILON)
        normed_ff = (middle * scale_second * gain_second).astype(jnp.bfloat16)
        rows_all = lax.all_gather(normed_ff, "shard", axis=0, tiled=True)
        gate = contract_last(rows_all, w_gate)
        upper = contract_last(rows_all, w_up)
        hidden = (gate * jax.nn.sigmoid(gate) * upper).astype(jnp.bfloat16)
        down_branch = lax.psum_scatter(
            jnp.dot(hidden, w_down, preferred_element_type=jnp.float32).astype(jnp.bfloat16),
            "shard",
            scatter_dimension=0,
            tiled=True,
        ).astype(jnp.float32)
        results.append((middle + RESIDUAL * down_branch).astype(jnp.bfloat16))
        cot = cotangent[batch_index, 0].astype(jnp.float32)
        down_grad = (RESIDUAL * cot).astype(jnp.bfloat16)
        cot_all = lax.all_gather(down_grad, "shard", axis=0, tiled=True)
        gate = contract_last(rows_all, w_gate)
        upper = contract_last(rows_all, w_up)
        sigma = jax.nn.sigmoid(gate)
        hidden = (gate * sigma * upper).astype(jnp.bfloat16)
        hidden_grad = contract_last(cot_all, w_down)
        gate_grad = (hidden_grad * upper * sigma * (1.0 + gate * (1.0 - sigma))).astype(
            jnp.bfloat16
        )
        up_grad = (hidden_grad * gate * sigma).astype(jnp.bfloat16)
        sums[6] = sums[6] + contract_first(gate_grad, rows_all)
        sums[7] = sums[7] + contract_first(up_grad, rows_all)
        sums[8] = sums[8] + contract_first(hidden, cot_all)
        ff_normed_grad = lax.psum_scatter(
            jnp.dot(gate_grad, w_gate, preferred_element_type=jnp.float32)
            + jnp.dot(up_grad, w_up, preferred_element_type=jnp.float32),
            "shard",
            scatter_dimension=0,
            tiled=True,
        )
        middle_back, gain_ff_term = norm_back(middle, scale_second, gain_second, ff_normed_grad)
        middle_grad = cot + middle_back
        out_grad = (RESIDUAL * middle_grad).astype(jnp.bfloat16)
        out_all = lax.all_gather(out_grad, "shard", axis=0, tiled=True)
        sums[4] = sums[4] + contract_first(attended_h, out_all)
        attended_grad = (
            contract_last(out_all, w_out)
            .astype(jnp.bfloat16)
            .reshape(tree_rows, own_heads, group, HEAD_DIM)
        )
        value_term = jnp.zeros((tree_rows, own_heads, HEAD_DIM), jnp.float32)
        key_term = jnp.zeros((tree_rows, own_heads, HEAD_DIM), jnp.float32)
        query_parts = []
        for block_index, begin in enumerate(range(0, tree_rows, block_rows)):
            query_blk = query_h[begin : begin + block_rows]
            grad_blk = attended_grad[begin : begin + block_rows]
            scores = (
                jnp.einsum("qhgd,khd->hgqk", query_blk, key_h, preferred_element_type=jnp.float32)
                * ATTN_SCALE
            )
            probs = jnp.exp(
                jnp.where(masks[block_index], scores, NEGATIVE) - log_totals[block_index]
            )
            probs_low = probs.astype(jnp.bfloat16)
            probs_grad = jnp.einsum(
                "qhgd,khd->hgqk", grad_blk, value_h, preferred_element_type=jnp.float32
            )
            value_term = value_term + jnp.einsum(
                "hgqk,qhgd->khd", probs_low, grad_blk, preferred_element_type=jnp.float32
            )
            score_grad = (
                probs * (probs_grad - jnp.sum(probs_grad * probs, axis=-1, keepdims=True))
            ).astype(jnp.bfloat16)
            query_parts.append(
                jnp.einsum("hgqk,khd->qhgd", score_grad, key_h, preferred_element_type=jnp.float32)
                * ATTN_SCALE
            )
            key_term = (
                key_term
                + jnp.einsum(
                    "hgqk,qhgd->khd", score_grad, query_blk, preferred_element_type=jnp.float32
                )
                * ATTN_SCALE
            )
        query_grad = jnp.concatenate(query_parts, axis=0)
        query_raw = rotate(
            query_grad.reshape(tree_rows, own_heads * group, HEAD_DIM), position_all, -1.0
        )
        query_raw = query_raw.reshape(tree_rows, own_heads * group * HEAD_DIM).astype(jnp.bfloat16)
        key_raw = (
            rotate(key_term, position_all, -1.0)
            .reshape(tree_rows, own_heads * HEAD_DIM)
            .astype(jnp.bfloat16)
        )
        value_raw = value_term.reshape(tree_rows, own_heads * HEAD_DIM).astype(jnp.bfloat16)
        sums[1] = sums[1] + contract_first(query_raw, normed_all)
        sums[2] = sums[2] + contract_first(key_raw, normed_all)
        sums[3] = sums[3] + contract_first(value_raw, normed_all)
        normed_grad = lax.psum_scatter(
            (
                jnp.dot(query_raw, w_query, preferred_element_type=jnp.float32)
                + jnp.dot(key_raw, w_key, preferred_element_type=jnp.float32)
                + jnp.dot(value_raw, w_value, preferred_element_type=jnp.float32)
            ).astype(jnp.bfloat16),
            "shard",
            scatter_dimension=0,
            tiled=True,
        ).astype(jnp.float32)
        input_back, gain_attn_term = norm_back(inputs, scale_first, gain_first, normed_grad)
        input_grads.append(middle_grad + input_back)
        gain_attn_acc = gain_attn_acc + gain_attn_term
        gain_ff_acc = gain_ff_acc + gain_ff_term
    owned_gains = (
        lax.psum_scatter(gain_attn_acc, "shard", scatter_dimension=0, tiled=True),
        lax.psum_scatter(gain_ff_acc, "shard", scatter_dimension=0, tiled=True),
    )
    sums[0] = owned_gains[0]
    sums[5] = owned_gains[1]
    totals = (
        lax.psum(sums[0].astype(jnp.bfloat16), "replica").astype(jnp.float32),
        lax.psum(sums[1].astype(jnp.bfloat16), "replica").astype(jnp.float32),
        lax.psum(sums[2].astype(jnp.bfloat16), "replica").astype(jnp.float32),
        lax.psum(sums[3].astype(jnp.bfloat16), "replica").astype(jnp.float32),
        lax.psum(sums[4].astype(jnp.bfloat16), "replica").astype(jnp.float32),
        lax.psum(sums[5].astype(jnp.bfloat16), "replica").astype(jnp.float32),
        lax.psum(sums[6].astype(jnp.bfloat16), "replica").astype(jnp.float32),
        lax.psum(sums[7].astype(jnp.bfloat16), "replica").astype(jnp.float32),
        lax.psum(sums[8].astype(jnp.bfloat16), "replica").astype(jnp.float32),
    )
    output = jnp.stack(results)[:, None]
    input_grad = jnp.stack(input_grads)[:, None]
    return (
        output,
        input_grad,
        totals[0],
        totals[1],
        totals[2],
        totals[3],
        totals[4],
        totals[5],
        totals[6],
        totals[7],
        totals[8],
    )


def solution(mesh):
    in_specs = (
        P(None, "replica", "shard", None),
        P("shard"),
        P("shard", None),
        P("shard", None),
        P("shard", None),
        P("shard", None),
        P("shard"),
        P("shard", None),
        P("shard", None),
        P("shard", None),
        P(None, "replica", "shard", None),
        P(None, "replica", "shard"),
        P(None, "replica", None),
    )
    out_specs = (
        P(None, "replica", "shard", None),
        P(None, "replica", "shard", None),
        P("shard"),
        P("shard", None),
        P("shard", None),
        P("shard", None),
        P("shard", None),
        P("shard"),
        P("shard", None),
        P("shard", None),
        P("shard", None),
    )
    return jax.shard_map(body, mesh=mesh, in_specs=in_specs, out_specs=out_specs, check_vma=False)
```

profile of v0, /device:TPU:0, one launch (start us, length us, event | category | flops | bytes accessed | tf_op | source)
XLA Modules:
  0.0 1901.9 jit_solution(17890299135495085045)
XLA Ops:
  44.1 32.7 %all-gather.15.cloned.1.call-done = bf16[1024,2048]{1,0:T(8,128)(2,1)} async-done(((bf16[256,2048]{1,0:T(8,128)(2,1)}), bf16[1024,2048]{1,0:T(8,128)(2,1)}) %all-gather.15.cloned.1.call-update) | async-done | bytes 4194320 | tf_op jit(solution)/shard_map/all_gather | solution.py:110
  229.1 89.6 %reduce-scatter.9.cloned.1.call-done = f32[256,2048]{1,0:T(8,128)} async-done(((f32[1024,2048]{1,0:T(8,128)}), f32[256,2048]{1,0:T(8,128)}) %reduce-scatter.9.cloned.1.call-update) | async-done | bytes 2097168 | tf_op jit(solution)/shard_map/reduce_scatter | solution.py:150
  329.8 49.3 %all-gather.13.cloned.1.call-done = bf16[1024,2048]{1,0:T(8,128)(2,1)} async-done(((bf16[256,2048]{1,0:T(8,128)(2,1)}), bf16[1024,2048]{1,0:T(8,128)(2,1)}) %all-gather.13.cloned.1.call-update) | async-done | bytes 4194320 | tf_op jit(solution)/shard_map/all_gather | solution.py:159
  379.1 15.9 fusion.186
  395.0 13.2 fusion.185
  408.2 25.9 %all-gather.19.cloned.1.call-done = bf16[1024,2048]{1,0:T(8,128)(2,1)} async-done(((bf16[256,2048]{1,0:T(8,128)(2,1)}), bf16[1024,2048]{1,0:T(8,128)(2,1)}) %all-gather.19.cloned.1.call-update) | async-done | bytes 4194320 | tf_op jit(solution)/shard_map/all_gather | solution.py:172
  434.1 22.0 %multiply_convert_fusion.2 = (bf16[1024,2048]{1,0:T(8,128)(2,1)}, bf16[1024,2048]{1,0:T(8,128)(2,1)}, bf16[1024,2048]{1,0:T(8,128)(2,1)}) fusion(f32[1024,2048]{1,0:T(8,128)} %fusion.185, f32[1024,2048]{1,0:T(8,128)} %fusion.186, bf16[1024,2048]{1,0:T(8,128)(2,1)} %all-gather.19.cloned.1.call-done, bf16[2048,2048]{1,0:T(8,128)(2,1)} %param.22), kind=kOutput, calls=%fused_computation.59 | convolution fusion | flops 8623489024 | bytes 41943040 | tf_op jit(solution)/shard_map/dot_general | solution.py:43
  456.1 12.6 fusion.191
  468.7 13.1 convolution_add_fusion.1
  482.2 86.3 %reduce-scatter.17.cloned.1.call-done = f32[256,2048]{1,0:T(8,128)} async-done(((f32[1024,2048]{1,0:T(8,128)}), f32[256,2048]{1,0:T(8,128)}) %reduce-scatter.17.cloned.1.call-update) | async-done | bytes 2097168 | tf_op jit(solution)/shard_map/reduce_scatter | solution.py:185
  574.4 52.1 %all-gather.17.cloned.1.call-done = bf16[1024,2048]{1,0:T(8,128)(2,1)} async-done(((bf16[256,2048]{1,0:T(8,128)(2,1)}), bf16[1024,2048]{1,0:T(8,128)(2,1)}) %all-gather.17.cloned.1.call-update) | async-done | bytes 4194320 | tf_op jit(solution)/shard_map/all_gather | solution.py:159
  626.4 15.5 fusion.190
  641.9 13.2 fusion.189
  655.1 26.0 %all-gather.23.cloned.1.call-done = bf16[1024,2048]{1,0:T(8,128)(2,1)} async-done(((bf16[256,2048]{1,0:T(8,128)(2,1)}), bf16[1024,2048]{1,0:T(8,128)(2,1)}) %all-gather.23.cloned.1.call-update) | async-done | bytes 4194320 | tf_op jit(solution)/shard_map/all_gather | solution.py:172
  681.2 22.3 %multiply_convert_fusion = (bf16[1024,2048]{1,0:T(8,128)(2,1)}, bf16[1024,2048]{1,0:T(8,128)(2,1)}, bf16[1024,2048]{1,0:T(8,128)(2,1)}) fusion(f32[1024,2048]{1,0:T(8,128)} %fusion.189, f32[1024,2048]{1,0:T(8,128)} %fusion.190, bf16[1024,2048]{1,0:T(8,128)(2,1)} %all-gather.23.cloned.1.call-done, bf16[2048,2048]{1,0:T(8,128)(2,1)} %param.22), kind=kOutput, calls=%fused_computation.54 | convolution fusion | flops 8623489024 | bytes 41943040 | tf_op jit(solution)/shard_map/dot_general | solution.py:43
  703.5 12.6 fusion.194
  716.1 13.3 convolution_add_fusion
  729.4 14.0 convolution_convert_fusion
  743.5 72.4 %reduce-scatter.21.cloned.1.call-done = f32[256,2048]{1,0:T(8,128)} async-done(((f32[1024,2048]{1,0:T(8,128)}), f32[256,2048]{1,0:T(8,128)}) %reduce-scatter.21.cloned.1.call-update) | async-done | bytes 2097168 | tf_op jit(solution)/shard_map/reduce_scatter | solution.py:185
  819.4 52.2 %reduce-scatter.15.cloned.1.call-done = bf16[256,2048]{1,0:T(8,128)(2,1)} async-done(((bf16[1024,2048]{1,0:T(8,128)(2,1)}), bf16[256,2048]{1,0:T(8,128)(2,1)}) %reduce-scatter.15.cloned.1.call-update) | async-done | bytes 1048592 | tf_op jit(solution)/shard_map/reduce_scatter | solution.py:163
  878.8 52.0 %all-gather.21.cloned.1.call-done = bf16[1024,2048]{1,0:T(8,128)(2,1)} async-done(((bf16[256,2048]{1,0:T(8,128)(2,1)}), bf16[1024,2048]{1,0:T(8,128)(2,1)}) %all-gather.21.cloned.1.call-update) | async-done | bytes 4194320 | tf_op jit(solution)/shard_map/all_gather | solution.py:195
  935.5 12.4 fusion.6
  1030.9 15.0 fusion
  1074.6 12.1 fusion.5
  1135.3 14.2 convolution_convert_fusion.1
  1149.6 15.8 fusion.202
  1188.9 16.2 add_convert_fusion
  1205.1 16.1 add_convert_fusion.1
  1221.2 16.3 add_convert_fusion.2
  1261.2 15.1 all-reduce.2
  1276.4 14.6 all-reduce.3
  1302.7 547.4 %all-reduce.7.cloned.1.call-done = (bf16[512,2048]{1,0:T(8,128)(2,1)}, bf16[128,2048]{1,0:T(8,128)(2,1)}, bf16[128,2048]{1,0:T(8,128)(2,1)}, bf16[512,2048]{1,0:...) async-done(((bf16[512,2048]{1,0:T(8,128)(2,1)}, bf16[128,2048]{1,0:T(8,128)(2,1)}, bf16[128,2048]{1,0:T(8,128)(2,1)}, ...) | async-done | bytes 30408720 | tf_op jit(solution)/shard_map/psum | solution.py:272
  (512 shorter events, 483.4 us)
Async XLA Ops:
  7.2 129.6 %copy-start = (bf16[512,2048]{1,0:T(8,128)(2,1)S(1)}, bf16[512,2048]{1,0:T(8,128)(2,1)}, u32[]{:S(2)}) copy-start(bf16[512,2048]{1,0:T(8,128)(2,1)} %param.18) | copy-start | bytes 6291460
  7.2 69.6 %all-gather.15.cloned.1.call-start = ((), (), s32[]{:S(2)}) async-start(), calls=%async_computation.12 | async-start | bytes 5242880 | tf_op jit(solution)/shard_map/all_gather | solution.py:110
  23.7 131.5 %all-gather.11.cloned.1.call-start = ((), (), s32[]{:S(2)}) async-start(), calls=%async_computation.8 | async-start | bytes 5242880 | tf_op jit(solution)/shard_map/all_gather | solution.py:110
  24.4 204.7 %reduce-scatter.13.cloned.1.call-start = ((), (), s32[]{:S(2)}) async-start(), calls=%async_computation.13 | async-start | bytes 10485760 | tf_op jit(solution)/shard_map/reduce_scatter | solution.py:150
  142.5 176.3 %reduce-scatter.9.cloned.1.call-start = ((), (), s32[]{:S(2)}) async-start(), calls=%async_computation.9 | async-start | bytes 10485760 | tf_op jit(solution)/shard_map/reduce_scatter | solution.py:150
  217.2 161.8 %all-gather.13.cloned.1.call-start = ((), (), s32[]{:S(2)}) async-start(), calls=%async_computation.10 | async-start | bytes 5242880 | tf_op jit(solution)/shard_map/all_gather | solution.py:159
  225.9 645.8 %copy-start.68 = (f32[4,1,512]{2,1,0:T(1,128)}, f32[4,1,512]{2,1,0:T(1,128)S(1)}, u32[]{:S(2)}) copy-start(f32[4,1,512]{2,1,0:T(1,128)S(1)} %convert_element_type.369) | copy-start | bytes 24580
  323.7 548.0 %copy-start.91 = (f32[256]{0:T(256)}, f32[256]{0:T(256)S(1)}, u32[]{:S(2)}) copy-start(f32[256]{0:T(256)S(1)} %add_rsqrt_fusion.2) | copy-start | bytes 3076
  326.2 107.8 %all-gather.19.cloned.1.call-start = ((), (), s32[]{:S(2)}) async-start(), calls=%async_computation.16 | async-start | bytes 5242880 | tf_op jit(solution)/shard_map/all_gather | solution.py:172
  329.7 238.8 %reduce-scatter.17.cloned.1.call-start = ((), (), s32[]{:S(2)}) async-start(), calls=%async_computation.17 | async-start | bytes 10485760 | tf_op jit(solution)/shard_map/reduce_scatter | solution.py:185
  481.9 144.6 %all-gather.17.cloned.1.call-start = ((), (), s32[]{:S(2)}) async-start(), calls=%async_computation.14 | async-start | bytes 5242880 | tf_op jit(solution)/shard_map/all_gather | solution.py:159
  482.2 389.5 %copy-start.89 = (f32[256]{0:T(256)}, f32[256]{0:T(256)S(1)}, u32[]{:S(2)}) copy-start(f32[256]{0:T(256)S(1)} %add_rsqrt_fusion) | copy-start | bytes 3076
  573.6 107.6 %all-gather.23.cloned.1.call-start = ((), (), s32[]{:S(2)}) async-start(), calls=%async_computation.20 | async-start | bytes 5242880 | tf_op jit(solution)/shard_map/all_gather | solution.py:172
  574.3 241.6 %reduce-scatter.21.cloned.1.call-start = ((), (), s32[]{:S(2)}) async-start(), calls=%async_computation.21 | async-start | bytes 10485760 | tf_op jit(solution)/shard_map/reduce_scatter | solution.py:185
  729.4 142.2 %reduce-scatter.15.cloned.1.call-start = ((), (), s32[]{:S(2)}) async-start(), calls=%async_computation.15 | async-start | bytes 5242880 | tf_op jit(solution)/shard_map/reduce_scatter | solution.py:163
  743.5 187.4 %all-gather.21.cloned.1.call-start = ((), (), s32[]{:S(2)}) async-start(), calls=%async_computation.18 | async-start | bytes 5242880 | tf_op jit(solution)/shard_map/all_gather | solution.py:195
  743.5 134.4 %copy-start.99 = (f32[256]{0:T(256)}, f32[256]{0:T(256)S(1)}, u32[]{:S(2)}) copy-start(f32[256]{0:T(256)S(1)} %broadcast_multiply_fusion.9) | copy-start | bytes 3076
  819.3 58.6 %copy-start.97 = (f32[256]{0:T(256)}, f32[256]{0:T(256)S(1)}, u32[]{:S(2)}) copy-start(f32[256]{0:T(256)S(1)} %broadcast_multiply_fusion.7) | copy-start | bytes 3076
  819.4 58.7 %copy-start.73 = (f32[2,4,512]{2,1,0:T(4,128)S(1)}, f32[2,4,512]{2,1,0:T(4,128)}, u32[]{:S(2)}) copy-start(f32[2,4,512]{2,1,0:T(4,128)} %copy-done.72) | copy-start | bytes 49156
  819.4 58.7 %copy-start.80 = (f32[2,4,512]{2,1,0:T(4,128)S(1)}, f32[2,4,512]{2,1,0:T(4,128)}, u32[]{:S(2)}) copy-start(f32[2,4,512]{2,1,0:T(4,128)} %fusion.15) | copy-start | bytes 49156
  819.4 58.7 %copy-start.75 = (f32[2,4,512]{2,1,0:T(4,128)S(1)}, f32[2,4,512]{2,1,0:T(4,128)}, u32[]{:S(2)}) copy-start(f32[2,4,512]{2,1,0:T(4,128)} %copy-done.74) | copy-start | bytes 49156
  819.4 58.7 %copy-start.82 = (f32[2,4,512]{2,1,0:T(4,128)S(1)}, f32[2,4,512]{2,1,0:T(4,128)}, u32[]{:S(2)}) copy-start(f32[2,4,512]{2,1,0:T(4,128)} %fusion.14) | copy-start | bytes 49156
  819.4 58.7 %copy-start.77 = (f32[2,4,512]{2,1,0:T(4,128)S(1)}, f32[2,4,512]{2,1,0:T(4,128)}, u32[]{:S(2)}) copy-start(f32[2,4,512]{2,1,0:T(4,128)} %copy-done.76) | copy-start | bytes 49156
  819.4 58.7 %copy-start.86 = (f32[2,4,512]{2,1,0:T(4,128)S(1)}, f32[2,4,512]{2,1,0:T(4,128)}, u32[]{:S(2)}) copy-start(f32[2,4,512]{2,1,0:T(4,128)} %copy-done.85) | copy-start | bytes 49156
  819.4 58.7 %copy-start.79 = (f32[2,4,512]{2,1,0:T(4,128)S(1)}, f32[2,4,512]{2,1,0:T(4,128)}, u32[]{:S(2)}) copy-start(f32[2,4,512]{2,1,0:T(4,128)} %copy-done.78) | copy-start | bytes 49156
  819.4 58.7 %copy-start.84 = (f32[2,4,512]{2,1,0:T(4,128)S(1)}, f32[2,4,512]{2,1,0:T(4,128)}, u32[]{:S(2)}) copy-start(f32[2,4,512]{2,1,0:T(4,128)} %copy-done.83) | copy-start | bytes 49156
  878.0 108.2 %all-gather.25.cloned.1.call-start = ((), (), s32[]{:S(2)}) async-start(), calls=%async_computation.22 | async-start | bytes 5242880 | tf_op jit(solution)/shard_map/all_gather | solution.py:195
  878.7 56.8 %copy-start.61 = (bf16[1024,128]{0,1:T(8,128)(2,1)S(1)}, bf16[1024,128]{0,1:T(8,128)(2,1)}, u32[]{:S(2)}) copy-start(bf16[1024,128]{0,1:T(8,128)(2,1)} %copy-done.60) | copy-start | bytes 786436
  878.7 379.5 %reduce-scatter.19.cloned.1.call-start = ((), (), s32[]{:S(2)}) async-start(), calls=%async_computation.19 | async-start | bytes 5242880 | tf_op jit(solution)/shard_map/reduce_scatter | solution.py:250
  1029.9 228.3 %reduce-scatter.23.cloned.1.call-start = ((), (), s32[]{:S(2)}) async-start(), calls=%async_computation.23 | async-start | bytes 5242880 | tf_op jit(solution)/shard_map/reduce_scatter | solution.py:250
  1135.2 156.9 %reduce-scatter.11.cloned.1.call-start = ((), (), s32[]{:S(2)}) async-start(), calls=%async_computation.11 | async-start | bytes 5242880 | tf_op jit(solution)/shard_map/reduce_scatter | solution.py:163
  1149.5 700.6 %all-reduce.7.cloned.1.call-start = ((), (), s32[]{:S(2)}) async-start(), calls=%async_computation.24 | async-start | bytes 60817408 | tf_op jit(solution)/shard_map/psum | solution.py:272
  (141 other events, 1202.0 us)
Sparse Core Ops, SparseCore 0:
  23.8 52.9 all-gather.14
  79.2 52.6 all-gather.10
  142.6 86.4 reduce-scatter.12
  232.4 86.3 reduce-scatter.8
  326.3 52.6 all-gather.12
  381.3 52.6 all-gather.18
  482.0 86.4 reduce-scatter.16
  573.7 52.6 all-gather.16
  628.4 52.6 all-gather.22
  729.5 86.4 reduce-scatter.20
  818.9 52.6 reduce-scatter.14
  878.1 52.6 all-gather.20
  933.4 52.6 all-gather.24
  1030.1 52.6 reduce-scatter.18
  1135.4 52.6 reduce-scatter.22
  1191.2 52.6 reduce-scatter.10
  1256.5 593.6 all-reduce.6
where the time goes:
time: 1910 us; the launch traced here: 1900 us
  waiting for transfers between devices  1100 us (58%)
  matrix products  510 us (27%)
  other arithmetic  179 us (9%)
  blocking collectives  55.1 us (3%)
  local copies, waits for them, and re-layouts  39.5 us (2%)
    psum x1, waiting for transfers between devices, body(): lax.psum(sums[1].astype(jnp.bfloat16), 'replica').astype(jnp.float32)  547 us
    reduce_scatter x2, waiting for transfers between devices, body(): lax.psum_scatter(jnp.dot(gate_grad, w_gate, preferred_element_type=jnp.fl...  159 us
    dot_general x14, matrix products, contract_last(): lax.dot_general(left, right, (((1,), (1,)), ((), ())), preferred_element_...  129 us
    dot_general x14, matrix products, contract_first(): lax.dot_general(left, right, (((0,), (0,)), ((), ())), preferred_element_...  104 us
    all_gather x2, waiting for transfers between devices, body(): rows_all = lax.all_gather(normed_ff, 'shard', axis=0, tiled=True)  101 us
    reduce_scatter x2, waiting for transfers between devices, body(): lax.psum_scatter(jnp.dot(attended_h, w_out, preferred_element_type=jnp.fl...  92.9 us
    all_gather x2, waiting for transfers between devices, body(): out_all = lax.all_gather(out_grad, 'shard', axis=0, tiled=True)  61 us
    reduce_scatter x2, waiting for transfers between devices, body(): lax.psum_scatter(jnp.dot(hidden, w_down, preferred_element_type=jnp.float...  52.2 us
  transfers between devices with their start and end apart: 17, of which 13 were waited for; matrix products, arithmetic and copies ran while one was open for 26% of the time, Pallas kernels for 0%

commit v1 on v0

--- a/solution.py
+++ b/solution.py
@@ -269,7 +269,9 @@
     sums[5] = owned_gains[1]
     totals = (
         lax.psum(sums[0].astype(jnp.bfloat16), "replica").astype(jnp.float32),
-        lax.psum(sums[1].astype(jnp.bfloat16), "replica").astype(jnp.float32),
+        jnp.sum(lax.all_gather(sums[1].astype(jnp.bfloat16), "replica"), axis=0).astype(
+            jnp.float32
+        ),
         lax.psum(sums[2].astype(jnp.bfloat16), "replica").astype(jnp.float32),
         lax.psum(sums[3].astype(jnp.bfloat16), "replica").astype(jnp.float32),
         lax.psum(sums[4].astype(jnp.bfloat16), "replica").astype(jnp.float32),

time: 1910 us -> 1980 us (1.037)
  waiting for transfers between devices: 1100 us -> 1160 us
    all_gather x0 -> x1, waiting for transfers between devices: none -> 110 us  [body(): lax.all_gather(sums[1].astype(jnp.bfloat16), 'replica')]
    psum x1, waiting for transfers between devices: 547 us -> 498 us  [body(): lax.psum(sums[2].astype(jnp.bfloat16), 'replica').astype(jnp.float32)]
  transfers between devices with their start and end apart: 17 -> 18, of which waited for: 13 -> 14; matrix products, arithmetic and copies ran while one was open for 26% -> 27% of each run, Pallas kernels for 0% -> 0%
where the time goes in v1:
time: 1980 us
  waiting for transfers between devices  1160 us (59%)
  matrix products  512 us (26%)
  other arithmetic  192 us (10%)
  blocking collectives  55.3 us (3%)
  local copies, waits for them, and re-layouts  40 us (2%)
    psum x1, waiting for transfers between devices, body(): lax.psum(sums[2].astype(jnp.bfloat16), 'replica').astype(jnp.float32)  498 us
    reduce_scatter x2, waiting for transfers between devices, body(): lax.psum_scatter(jnp.dot(gate_grad, w_gate, preferred_element_type=jnp.fl...  159 us
    dot_general x14, matrix products, contract_last(): lax.dot_general(left, right, (((1,), (1,)), ((), ())), preferred_element_...  129 us
    all_gather x1, waiting for transfers between devices, body(): lax.all_gather(sums[1].astype(jnp.bfloat16), 'replica')  110 us
    dot_general x14, matrix products, contract_first(): lax.dot_general(left, right, (((0,), (0,)), ((), ())), preferred_element_...  107 us
    all_gather x2, waiting for transfers between devices, body(): rows_all = lax.all_gather(normed_ff, 'shard', axis=0, tiled=True)  101 us
    reduce_scatter x2, waiting for transfers between devices, body(): lax.psum_scatter(jnp.dot(attended_h, w_out, preferred_element_type=jnp.fl...  92.9 us
    all_gather x2, waiting for transfers between devices, body(): out_all = lax.all_gather(out_grad, 'shard', axis=0, tiled=True)  61.3 us
  transfers between devices with their start and end apart: 18, of which 14 were waited for; matrix products, arithmetic and copies ran while one was open for 27% of the time, Pallas kernels for 0%

profile of v1, /device:TPU:0, one launch (start us, length us, event | category | flops | bytes accessed | tf_op | source)
XLA Modules:
  0.0 1979.4 jit_solution(11353267896459230729)
XLA Ops:
  44.1 32.7 %all-gather.17.cloned.1.call-done = bf16[1024,2048]{1,0:T(8,128)(2,1)} async-done(((bf16[256,2048]{1,0:T(8,128)(2,1)}), bf16[1024,2048]{1,0:T(8,128)(2,1)}) %all-gather.17.cloned.1.call-update) | async-done | bytes 4194320 | tf_op jit(solution)/shard_map/all_gather | solution.py:110
  229.0 89.6 %reduce-scatter.9.cloned.1.call-done = f32[256,2048]{1,0:T(8,128)} async-done(((f32[1024,2048]{1,0:T(8,128)}), f32[256,2048]{1,0:T(8,128)}) %reduce-scatter.9.cloned.1.call-update) | async-done | bytes 2097168 | tf_op jit(solution)/shard_map/reduce_scatter | solution.py:150
  329.6 49.3 %all-gather.15.cloned.1.call-done = bf16[1024,2048]{1,0:T(8,128)(2,1)} async-done(((bf16[256,2048]{1,0:T(8,128)(2,1)}), bf16[1024,2048]{1,0:T(8,128)(2,1)}) %all-gather.15.cloned.1.call-update) | async-done | bytes 4194320 | tf_op jit(solution)/shard_map/all_gather | solution.py:159
  378.9 15.7 fusion.186
  394.6 13.2 fusion.185
  407.9 26.1 %all-gather.21.cloned.1.call-done = bf16[1024,2048]{1,0:T(8,128)(2,1)} async-done(((bf16[256,2048]{1,0:T(8,128)(2,1)}), bf16[1024,2048]{1,0:T(8,128)(2,1)}) %all-gather.21.cloned.1.call-update) | async-done | bytes 4194320 | tf_op jit(solution)/shard_map/all_gather | solution.py:172
  433.9 22.3 %multiply_convert_fusion.2 = (bf16[1024,2048]{1,0:T(8,128)(2,1)}, bf16[1024,2048]{1,0:T(8,128)(2,1)}, bf16[1024,2048]{1,0:T(8,128)(2,1)}) fusion(f32[1024,2048]{1,0:T(8,128)} %fusion.185, f32[1024,2048]{1,0:T(8,128)} %fusion.186, bf16[1024,2048]{1,0:T(8,128)(2,1)} %all-gather.21.cloned.1.call-done, bf16[2048,2048]{1,0:T(8,128)(2,1)} %param.22), kind=kOutput, calls=%fused_computation.59 | convolution fusion | flops 8623489024 | bytes 41943040 | tf_op jit(solution)/shard_map/dot_general | solution.py:43
  456.2 12.6 fusion.191
  468.8 13.1 convolution_add_fusion.1
  482.2 86.3 %reduce-scatter.17.cloned.1.call-done = f32[256,2048]{1,0:T(8,128)} async-done(((f32[1024,2048]{1,0:T(8,128)}), f32[256,2048]{1,0:T(8,128)}) %reduce-scatter.17.cloned.1.call-update) | async-done | bytes 2097168 | tf_op jit(solution)/shard_map/reduce_scatter | solution.py:185
  574.4 52.1 %all-gather.19.cloned.1.call-done = bf16[1024,2048]{1,0:T(8,128)(2,1)} async-done(((bf16[256,2048]{1,0:T(8,128)(2,1)}), bf16[1024,2048]{1,0:T(8,128)(2,1)}) %all-gather.19.cloned.1.call-update) | async-done | bytes 4194320 | tf_op jit(solution)/shard_map/all_gather | solution.py:159
  626.5 15.5 fusion.190
  642.0 13.2 fusion.189
  655.2 26.0 %all-gather.25.cloned.1.call-done = bf16[1024,2048]{1,0:T(8,128)(2,1)} async-done(((bf16[256,2048]{1,0:T(8,128)(2,1)}), bf16[1024,2048]{1,0:T(8,128)(2,1)}) %all-gather.25.cloned.1.call-update) | async-done | bytes 4194320 | tf_op jit(solution)/shard_map/all_gather | solution.py:172
  681.2 22.1 %multiply_convert_fusion = (bf16[1024,2048]{1,0:T(8,128)(2,1)}, bf16[1024,2048]{1,0:T(8,128)(2,1)}, bf16[1024,2048]{1,0:T(8,128)(2,1)}) fusion(f32[1024,2048]{1,0:T(8,128)} %fusion.189, f32[1024,2048]{1,0:T(8,128)} %fusion.190, bf16[1024,2048]{1,0:T(8,128)(2,1)} %all-gather.25.cloned.1.call-done, bf16[2048,2048]{1,0:T(8,128)(2,1)} %param.22), kind=kOutput, calls=%fused_computation.54 | convolution fusion | flops 8623489024 | bytes 41943040 | tf_op jit(solution)/shard_map/dot_general | solution.py:43
  703.3 12.6 fusion.194
  716.0 13.3 convolution_add_fusion
  729.3 14.2 convolution_convert_fusion
  743.6 72.2 %reduce-scatter.21.cloned.1.call-done = f32[256,2048]{1,0:T(8,128)} async-done(((f32[1024,2048]{1,0:T(8,128)}), f32[256,2048]{1,0:T(8,128)}) %reduce-scatter.21.cloned.1.call-update) | async-done | bytes 2097168 | tf_op jit(solution)/shard_map/reduce_scatter | solution.py:185
  819.3 52.2 %reduce-scatter.15.cloned.1.call-done = bf16[256,2048]{1,0:T(8,128)(2,1)} async-done(((bf16[1024,2048]{1,0:T(8,128)(2,1)}), bf16[256,2048]{1,0:T(8,128)(2,1)}) %reduce-scatter.15.cloned.1.call-update) | async-done | bytes 1048592 | tf_op jit(solution)/shard_map/reduce_scatter | solution.py:163
  878.7 52.0 %all-gather.23.cloned.1.call-done = bf16[1024,2048]{1,0:T(8,128)(2,1)} async-done(((bf16[256,2048]{1,0:T(8,128)(2,1)}), bf16[1024,2048]{1,0:T(8,128)(2,1)}) %all-gather.23.cloned.1.call-update) | async-done | bytes 4194320 | tf_op jit(solution)/shard_map/all_gather | solution.py:195
  1030.7 15.0 fusion
  1135.1 14.1 convolution_convert_fusion.1
  1149.2 15.8 fusion.202
  1188.5 16.5 add_convert_fusion
  1205.1 16.1 add_convert_fusion.1
  1221.2 16.2 add_convert_fusion.2
  1264.2 15.1 all-reduce.2
  1279.5 14.6 all-reduce.3
  1305.6 498.3 %all-reduce.7.cloned.1.call-done = (bf16[128,2048]{1,0:T(8,128)(2,1)}, bf16[128,2048]{1,0:T(8,128)(2,1)}, bf16[512,2048]{1,0:T(8,128)(2,1)}, bf16[2048,2048]{1,0...) async-done(((bf16[128,2048]{1,0:T(8,128)(2,1)}, bf16[128,2048]{1,0:T(8,128)(2,1)}, bf16[512,2048]{1,0:T(8,128)(2,1)}, bf16[2048,2048]{1,0:T(8,128)(2,1)}, ...) | async-done | bytes 28311568 | tf_op jit(solution)/shard_map/psum | solution.py:275
  1810.9 12.6 convert_element_type.361
  1847.1 110.2 %all-gather.29.cloned.1.call-done = bf16[4096,2048]{1,0:T(8,128)(2,1)} async-done(((bf16[512,2048]{1,0:T(8,128)(2,1)}), bf16[4096,2048]{1,0:T(8,128)(2,1)}) %all-gather.29.cloned.1.call-update) | async-done | bytes 16777232 | tf_op jit(solution)/shard_map/all_gather | solution.py:272
  (516 shorter events, 511.3 us)
Async XLA Ops:
  7.2 129.4 %copy-start = (bf16[512,2048]{1,0:T(8,128)(2,1)S(1)}, bf16[512,2048]{1,0:T(8,128)(2,1)}, u32[]{:S(2)}) copy-start(bf16[512,2048]{1,0:T(8,128)(2,1)} %param.18) | copy-start | bytes 6291460
  7.2 69.6 %all-gather.17.cloned.1.call-start = ((), (), s32[]{:S(2)}) async-start(), calls=%async_computation.12 | async-start | bytes 5242880 | tf_op jit(solution)/shard_map/all_gather | solution.py:110
  23.7 131.5 %all-gather.13.cloned.1.call-start = ((), (), s32[]{:S(2)}) async-start(), calls=%async_computation.8 | async-start | bytes 5242880 | tf_op jit(solution)/shard_map/all_gather | solution.py:110
  24.4 204.6 %reduce-scatter.13.cloned.1.call-start = ((), (), s32[]{:S(2)}) async-start(), calls=%async_computation.13 | async-start | bytes 10485760 | tf_op jit(solution)/shard_map/reduce_scatter | solution.py:150
  142.3 176.3 %reduce-scatter.9.cloned.1.call-start = ((), (), s32[]{:S(2)}) async-start(), calls=%async_computation.9 | async-start | bytes 10485760 | tf_op jit(solution)/shard_map/reduce_scatter | solution.py:150
  217.1 161.8 %all-gather.15.cloned.1.call-start = ((), (), s32[]{:S(2)}) async-start(), calls=%async_computation.10 | async-start | bytes 5242880 | tf_op jit(solution)/shard_map/all_gather | solution.py:159
  225.8 645.8 %copy-start.68 = (f32[4,1,512]{2,1,0:T(1,128)}, f32[4,1,512]{2,1,0:T(1,128)S(1)}, u32[]{:S(2)}) copy-start(f32[4,1,512]{2,1,0:T(1,128)S(1)} %convert_element_type.371) | copy-start | bytes 24580
  323.5 548.0 %copy-start.91 = (f32[256]{0:T(256)}, f32[256]{0:T(256)S(1)}, u32[]{:S(2)}) copy-start(f32[256]{0:T(256)S(1)} %add_rsqrt_fusion.2) | copy-start | bytes 3076
  326.1 107.9 %all-gather.21.cloned.1.call-start = ((), (), s32[]{:S(2)}) async-start(), calls=%async_computation.16 | async-start | bytes 5242880 | tf_op jit(solution)/shard_map/all_gather | solution.py:172
  329.6 239.0 %reduce-scatter.17.cloned.1.call-start = ((), (), s32[]{:S(2)}) async-start(), calls=%async_computation.17 | async-start | bytes 10485760 | tf_op jit(solution)/shard_map/reduce_scatter | solution.py:185
  482.0 144.5 %all-gather.19.cloned.1.call-start = ((), (), s32[]{:S(2)}) async-start(), calls=%async_computation.14 | async-start | bytes 5242880 | tf_op jit(solution)/shard_map/all_gather | solution.py:159
  482.2 389.3 %copy-start.89 = (f32[256]{0:T(256)}, f32[256]{0:T(256)S(1)}, u32[]{:S(2)}) copy-start(f32[256]{0:T(256)S(1)} %add_rsqrt_fusion) | copy-start | bytes 3076
  573.7 107.6 %all-gather.25.cloned.1.call-start = ((), (), s32[]{:S(2)}) async-start(), calls=%async_computation.20 | async-start | bytes 5242880 | tf_op jit(solution)/shard_map/all_gather | solution.py:172
  574.4 241.5 %reduce-scatter.21.cloned.1.call-start = ((), (), s32[]{:S(2)}) async-start(), calls=%async_computation.21 | async-start | bytes 10485760 | tf_op jit(solution)/shard_map/reduce_scatter | solution.py:185
  729.3 142.3 %reduce-scatter.15.cloned.1.call-start = ((), (), s32[]{:S(2)}) async-start(), calls=%async_computation.15 | async-start | bytes 5242880 | tf_op jit(solution)/shard_map/reduce_scatter | solution.py:163
  743.6 187.2 %all-gather.23.cloned.1.call-start = ((), (), s32[]{:S(2)}) async-start(), calls=%async_computation.18 | async-start | bytes 5242880 | tf_op jit(solution)/shard_map/all_gather | solution.py:195
  743.6 134.2 %copy-start.99 = (f32[256]{0:T(256)}, f32[256]{0:T(256)S(1)}, u32[]{:S(2)}) copy-start(f32[256]{0:T(256)S(1)} %broadcast_multiply_fusion.9) | copy-start | bytes 3076
  819.2 58.6 %copy-start.97 = (f32[256]{0:T(256)}, f32[256]{0:T(256)S(1)}, u32[]{:S(2)}) copy-start(f32[256]{0:T(256)S(1)} %broadcast_multiply_fusion.7) | copy-start | bytes 3076
  819.2 58.7 %copy-start.73 = (f32[2,4,512]{2,1,0:T(4,128)S(1)}, f32[2,4,512]{2,1,0:T(4,128)}, u32[]{:S(2)}) copy-start(f32[2,4,512]{2,1,0:T(4,128)} %copy-done.72) | copy-start | bytes 49156
  819.2 58.7 %copy-start.80 = (f32[2,4,512]{2,1,0:T(4,128)S(1)}, f32[2,4,512]{2,1,0:T(4,128)}, u32[]{:S(2)}) copy-start(f32[2,4,512]{2,1,0:T(4,128)} %fusion.15) | copy-start | bytes 49156
  819.3 58.7 %copy-start.75 = (f32[2,4,512]{2,1,0:T(4,128)S(1)}, f32[2,4,512]{2,1,0:T(4,128)}, u32[]{:S(2)}) copy-start(f32[2,4,512]{2,1,0:T(4,128)} %copy-done.74) | copy-start | bytes 49156
  819.3 58.7 %copy-start.82 = (f32[2,4,512]{2,1,0:T(4,128)S(1)}, f32[2,4,512]{2,1,0:T(4,128)}, u32[]{:S(2)}) copy-start(f32[2,4,512]{2,1,0:T(4,128)} %fusion.14) | copy-start | bytes 49156
  819.3 58.7 %copy-start.77 = (f32[2,4,512]{2,1,0:T(4,128)S(1)}, f32[2,4,512]{2,1,0:T(4,128)}, u32[]{:S(2)}) copy-start(f32[2,4,512]{2,1,0:T(4,128)} %copy-done.76) | copy-start | bytes 49156
  819.3 58.7 %copy-start.86 = (f32[2,4,512]{2,1,0:T(4,128)S(1)}, f32[2,4,512]{2,1,0:T(4,128)}, u32[]{:S(2)}) copy-start(f32[2,4,512]{2,1,0:T(4,128)} %copy-done.85) | copy-start | bytes 49156
  819.3 58.7 %copy-start.79 = (f32[2,4,512]{2,1,0:T(4,128)S(1)}, f32[2,4,512]{2,1,0:T(4,128)}, u32[]{:S(2)}) copy-start(f32[2,4,512]{2,1,0:T(4,128)} %copy-done.78) | copy-start | bytes 49156
  819.3 58.7 %copy-start.84 = (f32[2,4,512]{2,1,0:T(4,128)S(1)}, f32[2,4,512]{2,1,0:T(4,128)}, u32[]{:S(2)}) copy-start(f32[2,4,512]{2,1,0:T(4,128)} %copy-done.83) | copy-start | bytes 49156
  877.9 108.2 %all-gather.27.cloned.1.call-start = ((), (), s32[]{:S(2)}) async-start(), calls=%async_computation.22 | async-start | bytes 5242880 | tf_op jit(solution)/shard_map/all_gather | solution.py:195
  878.6 382.6 %reduce-scatter.19.cloned.1.call-start = ((), (), s32[]{:S(2)}) async-start(), calls=%async_computation.19 | async-start | bytes 5242880 | tf_op jit(solution)/shard_map/reduce_scatter | solution.py:250
  1029.8 231.5 %reduce-scatter.23.cloned.1.call-start = ((), (), s32[]{:S(2)}) async-start(), calls=%async_computation.23 | async-start | bytes 5242880 | tf_op jit(solution)/shard_map/reduce_scatter | solution.py:250
  1135.0 160.3 %reduce-scatter.11.cloned.1.call-start = ((), (), s32[]{:S(2)}) async-start(), calls=%async_computation.11 | async-start | bytes 5242880 | tf_op jit(solution)/shard_map/reduce_scatter | solution.py:163
  1149.1 654.8 %all-reduce.7.cloned.1.call-start = ((), (), s32[]{:S(2)}) async-start(), calls=%async_computation.25 | async-start | bytes 56623104 | tf_op jit(solution)/shard_map/psum | solution.py:275
  1250.3 707.0 %all-gather.29.cloned.1.call-start = ((), (), s32[]{:S(2)}) async-start(), calls=%async_computation.24 | async-start | bytes 18874368 | tf_op jit(solution)/shard_map/all_gather | solution.py:272
  (142 other events, 1282.0 us)
Sparse Core Ops, SparseCore 0:
  23.8 52.9 all-gather.16
  79.2 52.6 all-gather.12
  142.4 86.5 reduce-scatter.12
  232.2 86.3 reduce-scatter.8
  326.2 52.6 all-gather.14
  381.2 52.6 all-gather.20
  482.1 86.3 reduce-scatter.16
  573.8 52.6 all-gather.18
  628.5 52.6 all-gather.24
  729.4 86.4 reduce-scatter.20
  818.8 52.6 reduce-scatter.14
  878.0 52.6 all-gather.22
  933.3 52.6 all-gather.26
  1029.9 52.6 reduce-scatter.18
  1135.1 52.6 reduce-scatter.22
  1190.9 52.6 reduce-scatter.10
  1250.4 553.5 all-reduce.6
  1806.0 151.2 all-gather.28
